TPU v7x, 256 devices: a whole 4x4x8 slice. The times are simulated.
256 devices in a mesh: ctx: 32 (over x, z), ch: 8 (over y, core).
Axes of the slice: x: 4, y: 4, z: 8, core: 2. Of those that a mesh axis runs over, the one named last changes fastest.
Arguments:
- tokens: bfloat16 [32768, 8192], P('ctx', 'ch'), may hold values from -6 to 6
- in_proj: bfloat16 [3, 8192, 256], P(None, 'ch'), may hold values from -0.09375 to 0.09375
- short_taps: float32 [256, 3, 3], P('ch'), may hold values from -3.5 to 3.5
- long_filter: float32 [256, 32768], P('ch', 'ctx'), may hold values from -4 to 4
- skip_gain: float32 [256], P('ch'), may hold values from 0.5 to 1.5
- out_proj: bfloat16 [256, 8192], P(None, 'ch'), may hold values from -0.375 to 0.375
Outputs:
- operator_out: bfloat16 [32768, 8192], P('ctx', 'ch')
All inputs are finite; a program needn't handle non-finite values.
Results may differ from a plain program's by a relative error of at most 0.0049.
Values may be sent and summed in bfloat16 or wider, within the bound.
A program may use at most 64 MiB of HBM per device.

v0:
```python
import math

import jax
import jax.numpy as jnp
from jax import lax
from jax.sharding import PartitionSpec as P

SHORT = 3


TWO_PI = 2.0 * math.pi
HIGHEST = lax.Precision.HIGHEST


def from_partner(value, axis, stride):
    return lax.ppermute(value, axis, [(i, i ^ 1 << stride) for i in range(lax.axis_size(axis))])


def from_behind(block, axis, distance):
    devices = range(lax.axis_size(axis))
    route = [(i - distance, i) for i in devices if i - distance in devices]
    return lax.ppermute(block, axis, route)


def angle_table(outer, inner, period, orient):
    phase = outer[:, None] * inner[None, :] % period
    angle = orient * TWO_PI / period * phase.astype(jnp.float32)
    return (jnp.cos(angle), jnp.sin(angle))


def complex_apply(real_part, imag_part, cos_table, sin_table, pattern):

    def multiply(left, table):
        return jnp.einsum(pattern, left, table, precision=HIGHEST)

    return (
        multiply(real_part, cos_table) - multiply(imag_part, sin_table),
        multiply(real_part, sin_table) + multiply(imag_part, cos_table),
    )


def finish_forward(real_part, imag_part, block_index, full_length):
    tok_rows = real_part.shape[-1]
    sample_offsets = jnp.arange(tok_rows, dtype=jnp.int32)
    freq_low = 2 * block_index + jnp.arange(2, dtype=jnp.int32)
    twist_cos, twist_sin = angle_table(freq_low, sample_offsets, full_length, -1.0)
    twisted_re = real_part * twist_cos - imag_part * twist_sin
    twisted_im = real_part * twist_sin + imag_part * twist_cos
    dft_cos, dft_sin = angle_table(sample_offsets, sample_offsets, tok_rows, -1.0)
    return complex_apply(twisted_re, twisted_im, dft_cos, dft_sin, "...n,nk->...k")


def start_inverse(real_part, imag_part, block_index, full_length):
    tok_rows = real_part.shape[-1]
    sample_offsets = jnp.arange(tok_rows, dtype=jnp.int32)
    dft_cos, dft_sin = angle_table(sample_offsets, sample_offsets, tok_rows, 1.0)
    local_re, local_im = complex_apply(real_part, imag_part, dft_cos, dft_sin, "...k,kn->...n")
    freq_low = 2 * block_index + jnp.arange(2, dtype=jnp.int32)
    twist_cos, twist_sin = angle_table(freq_low, sample_offsets, full_length, 1.0)
    return (
        local_re * twist_cos - local_im * twist_sin,
        local_re * twist_sin + local_im * twist_cos,
    )


def forward_butterfly(signals, size_ctx, index_ctx):
    base = TWO_PI * 0.5 / size_ctx * index_ctx.astype(jnp.float32)
    real_part = jnp.stack([signals, signals * jnp.cos(base)], axis=2)
    imag_part = jnp.stack([jnp.zeros_like(signals), -signals * jnp.sin(base)], axis=2)
    levels = size_ctx.bit_length() - 1
    block_index = jnp.zeros((), jnp.int32)
    for section in reversed(range(levels)):
        half = 1 << section
        other_re, other_im = from_partner((real_part, imag_part), "ctx", section)
        upper = index_ctx >> section & 1 == 0
        theta = -TWO_PI / (2 * half) * (index_ctx % half).astype(jnp.float32)
        wave_cos, wave_sin = (jnp.cos(theta), jnp.sin(theta))
        diff_re = other_re - real_part
        diff_im = other_im - imag_part
        lower_re = diff_re * wave_cos - diff_im * wave_sin
        lower_im = diff_re * wave_sin + diff_im * wave_cos
        real_part = jnp.where(upper, real_part + other_re, lower_re)
        imag_part = jnp.where(upper, imag_part + other_im, lower_im)
    for section in range(levels):
        block_index = block_index + ((index_ctx >> section & 1) << levels - 1 - section)
    return (real_part, imag_part, block_index)


def inverse_butterfly(real_part, imag_part, size_ctx, index_ctx):
    levels = size_ctx.bit_length() - 1
    for section in range(levels):
        half = 1 << section
        other_re, other_im = from_partner((real_part, imag_part), "ctx", section)
        upper = index_ctx >> section & 1 == 0
        theta = TWO_PI / (2 * half) * (index_ctx % half).astype(jnp.float32)
        wave_cos, wave_sin = (jnp.cos(theta), jnp.sin(theta))
        turned_other_re = other_re * wave_cos - other_im * wave_sin
        turned_other_im = other_re * wave_sin + other_im * wave_cos
        turned_self_re = real_part * wave_cos - imag_part * wave_sin
        turned_self_im = real_part * wave_sin + imag_part * wave_cos
        real_part, imag_part = (
            jnp.where(upper, real_part + turned_other_re, other_re - turned_self_re),
            jnp.where(upper, imag_part + turned_other_im, other_im - turned_self_im),
        )
    base = TWO_PI * 0.5 / size_ctx * index_ctx.astype(jnp.float32)
    return real_part[:, 0] + real_part[:, 1] * jnp.cos(base) - imag_part[:, 1] * jnp.sin(base)


def per_device(tokens, in_proj, short_taps, long_filter, skip_gain, out_proj):
    tok_rows = tokens.shape[0]
    size_ctx = lax.axis_size("ctx")
    index_ctx = lax.axis_index("ctx")
    full_length = 2 * size_ctx * tok_rows
    projected = lax.psum_scatter(
        jnp.einsum("td,jdc->cjt", tokens, in_proj, preferred_element_type=jnp.float32),
        "ch",
        scatter_dimension=0,
        tiled=True,
    )
    rim = from_behind(projected[:, :, tok_rows - (SHORT - 1) :], "ctx", 1)
    extended = jnp.concatenate([rim, projected], axis=2)
    featured = jnp.zeros_like(projected)
    for lag in range(SHORT):
        featured = (
            featured
            + short_taps[:, :, lag, None]
            * extended[:, :, SHORT - 1 - lag : SHORT - 1 - lag + tok_rows]
        )
    outer_gate = featured[:, 0]
    carried = featured[:, 1] * featured[:, 2]
    signals = jnp.stack([carried, long_filter], axis=0)
    partial_re, partial_im, block_index = forward_butterfly(signals, size_ctx, index_ctx)
    spec_re, spec_im = finish_forward(partial_re, partial_im, block_index, full_length)
    scale = 1.0 / full_length
    product_re = (spec_re[0] * spec_re[1] - spec_im[0] * spec_im[1]) * scale
    product_im = (spec_re[0] * spec_im[1] + spec_im[0] * spec_re[1]) * scale
    back_re, back_im = start_inverse(product_re, product_im, block_index, full_length)
    convolved = inverse_butterfly(back_re, back_im, size_ctx, index_ctx)
    gated = (outer_gate * (convolved + skip_gain[:, None] * carried)).astype(jnp.bfloat16)
    summed = jnp.einsum(
        "ct,cd->td",
        lax.all_gather(gated, "ch", axis=0, tiled=True),
        out_proj,
        preferred_element_type=jnp.float32,
    )
    return summed.astype(jnp.bfloat16)


def solution(mesh):
    placed = (
        P("ctx", "ch"),
        P(None, "ch", None),
        P("ch", None, None),
        P("ch", "ctx"),
        P("ch"),
        P(None, "ch"),
    )
    return jax.shard_map(
        per_device, mesh=mesh, in_specs=placed, out_specs=P("ctx", "ch"), check_vma=False
    )
```

profile of v0, /device:TPU:1, one launch (start us, length us, event | category | flops | bytes accessed | tf_op | source)
XLA Modules:
  0.0 516.5 jit_solution(13787650287794628605)
XLA Ops:
  8.1 4.9 fusion.39
  13.7 38.8 %reduce-scatter.2.cloned.1.call-done = f32[32,3,1024]{2,0,1:T(8,128)} async-done(((f32[256,3,1024]{2,0,1:T(8,128)}), f32[32,3,1024]{2,0,1:T(8,128)}) %reduce-scatter.2.cloned.1.call-update) | async-done | bytes 393232 | tf_op jit(solution)/shard_map/reduce_scatter | solution.py:114
  60.2 5.3 %collective-permute-start.1 = (f32[2,32,2,1024]{3,1,2,0:T(8,128)}, f32[2,32,2,1024]{3,1,2,0:T(8,128)}, u32[]{:S(2)}, u32[]{:S(2)}) collective-permute-start(f32[2,32,2,1024]{3,1,2,0:T(8,128)} %pad_maximum_fusion), channel_id=1, source_target_pairs={{0,128},{8,136},{16,144},{24,152},{32,160},{40,168},{48,176},{56,1... | collective-permute-start | bytes 1572872 | tf_op jit(solution)/shard_map/ppermute | solution.py:16
  66.5 6.7 %collective-permute-done.1 = f32[2,32,2,1024]{3,1,2,0:T(8,128)} collective-permute-done((f32[2,32,2,1024]{3,1,2,0:T(8,128)}, f32[2,32,2,1024]{3,1,2,0:T(8,128)}, u32[]{:S(2)}, u32[]{:S(2)}) %collective-permute-start.1) | collective-permute-done | bytes 524320 | tf_op jit(solution)/shard_map/ppermute | solution.py:16
  73.2 11.2 %collective-permute-done.2 = f32[2,32,2,1024]{3,1,2,0:T(8,128)} collective-permute-done((f32[2,32,2,1024]{3,1,2,0:T(8,128)}, f32[2,32,2,1024]{3,1,2,0:T(8,128)}, u32[]{:S(2)}, u32[]{:S(2)}) %collective-permute-start.2) | collective-permute-done | bytes 524320 | tf_op jit(solution)/shard_map/ppermute | solution.py:16
  88.5 6.6 %collective-permute-done.3 = f32[2,32,2,1024]{3,1,2,0:T(8,128)S(1)} collective-permute-done((f32[2,32,2,1024]{3,1,2,0:T(8,128)}, f32[2,32,2,1024]{3,1,2,0:T(8,128)S(1)}, u32[]{:S(2)}, u32[]{:S(2)}) %collective-permute-start.3) | collective-permute-done | bytes 524320 | tf_op jit(solution)/shard_map/ppermute | solution.py:16
  95.9 10.4 %collective-permute-done.4 = f32[2,32,2,1024]{3,1,2,0:T(8,128)} collective-permute-done((f32[2,32,2,1024]{3,1,2,0:T(8,128)}, f32[2,32,2,1024]{3,1,2,0:T(8,128)}, u32[]{:S(2)}, u32[]{:S(2)}) %collective-permute-start.4) | collective-permute-done | bytes 524320 | tf_op jit(solution)/shard_map/ppermute | solution.py:16
  113.7 28.8 %collective-permute-done.5 = f32[2,32,2,1024]{3,1,2,0:T(8,128)} collective-permute-done((f32[2,32,2,1024]{3,1,2,0:T(8,128)S(1)}, f32[2,32,2,1024]{3,1,2,0:T(8,128)}, u32[]{:S(2)}, u32[]{:S(2)}) %collective-permute-start.5) | collective-permute-done | bytes 524320 | tf_op jit(solution)/shard_map/ppermute | solution.py:16
  142.5 14.7 %collective-permute-done.6 = f32[2,32,2,1024]{3,1,2,0:T(8,128)} collective-permute-done((f32[2,32,2,1024]{3,1,2,0:T(8,128)S(1)}, f32[2,32,2,1024]{3,1,2,0:T(8,128)}, u32[]{:S(2)}, u32[]{:S(2)}) %collective-permute-start.6) | collective-permute-done | bytes 524320 | tf_op jit(solution)/shard_map/ppermute | solution.py:16
  161.6 34.3 %collective-permute-done.7 = f32[2,32,2,1024]{3,1,2,0:T(8,128)} collective-permute-done((f32[2,32,2,1024]{3,1,2,0:T(8,128)S(1)}, f32[2,32,2,1024]{3,1,2,0:T(8,128)}, u32[]{:S(2)}, u32[]{:S(2)}) %collective-permute-start.7) | collective-permute-done | bytes 524320 | tf_op jit(solution)/shard_map/ppermute | solution.py:16
  195.9 11.2 %collective-permute-done.8 = f32[2,32,2,1024]{3,1,2,0:T(8,128)} collective-permute-done((f32[2,32,2,1024]{3,1,2,0:T(8,128)S(1)}, f32[2,32,2,1024]{3,1,2,0:T(8,128)}, u32[]{:S(2)}, u32[]{:S(2)}) %collective-permute-start.8) | collective-permute-done | bytes 524320 | tf_op jit(solution)/shard_map/ppermute | solution.py:16
  211.5 11.3 %collective-permute-done.9 = f32[2,32,2,1024]{3,1,2,0:T(8,128)S(1)} collective-permute-done((f32[2,32,2,1024]{3,1,2,0:T(8,128)}, f32[2,32,2,1024]{3,1,2,0:T(8,128)S(1)}, u32[]{:S(2)}, u32[]{:S(2)}) %collective-permute-start.9) | collective-permute-done | bytes 524320 | tf_op jit(solution)/shard_map/ppermute | solution.py:16
  222.8 11.2 %collective-permute-done.10 = f32[2,32,2,1024]{3,1,2,0:T(8,128)S(1)} collective-permute-done((f32[2,32,2,1024]{3,1,2,0:T(8,128)}, f32[2,32,2,1024]{3,1,2,0:T(8,128)S(1)}, u32[]{:S(2)}, u32[]{:S(2)}) %collective-permute-start.10) | collective-permute-done | bytes 524320 | tf_op jit(solution)/shard_map/ppermute | solution.py:16
  235.4 18.4 %fusion.10 = f32[2,32,2,1024]{3,1,2,0:T(8,128)S(1)} fusion(f32[2,32,2,1024]{3,1,2,0:T(8,128)S(1)} %get-tuple-element.6, f32[2,32,2,1024]{3,1,2,0:T(8,128)S(1)} %get-tuple-element.5, f32[2,1024]{1,0:T(2,128)S(1)} %get-tuple-element.36, f32[2,1024]{1,0:T(2,128)S(1)} %get-tuple-element.37), kind=kOutput, calls=%fused_computation.13 | convolution fusion | flops 1625686016 | bytes 1589248 | tf_op jit(solution)/shard_map/...n,nk->...k/dot_general | solution.py:34
  253.8 18.5 %fusion.16 = f32[2,32,2,1024]{3,1,2,0:T(8,128)S(1)} fusion(f32[2,32,2,1024]{3,1,2,0:T(8,128)S(1)} %get-tuple-element.6, f32[2,32,2,1024]{3,1,2,0:T(8,128)S(1)} %get-tuple-element.5, f32[2,1024]{1,0:T(2,128)S(1)} %get-tuple-element.36, f32[2,1024]{1,0:T(2,128)S(1)} %get-tuple-element.37), kind=kOutput, calls=%fused_computation.19 | convolution fusion | flops 1625686016 | bytes 1589248 | tf_op jit(solution)/shard_map/...n,nk->...k/dot_general | solution.py:34
  272.3 18.7 %fusion.42 = f32[2,32,2,1024]{3,1,2,0:T(8,128)S(1)} fusion(f32[2,32,2,1024]{3,1,2,0:T(8,128)S(1)} %fusion.10, f32[2,32,2,1024]{3,1,2,0:T(8,128)S(1)} %get-tuple-element.6, f32[2,32,2,1024]{3,1,2,0:T(8,128)S(1)} %get-tuple-element.5, f32[2,1024]{1,0:T(2,128)S(1)} %get-tuple-element.36, f32[2,1024]{1,0:T(2,128)S(1)} %get-tuple-element.37), kind=kOutput, calls=%fused_computation.40 | convolution fusion | flops 1625817088 | bytes 2113536 | tf_op jit(solution)/shard_map/...n,nk->...k/dot_general | solution.py:34
  291.0 18.3 %fusion.45 = f32[2,32,2,1024]{3,1,2,0:T(8,128)S(1)} fusion(f32[2,32,2,1024]{3,1,2,0:T(8,128)S(1)} %fusion.16, f32[2,32,2,1024]{3,1,2,0:T(8,128)S(1)} %get-tuple-element.6, f32[2,32,2,1024]{3,1,2,0:T(8,128)S(1)} %get-tuple-element.5, f32[2,1024]{1,0:T(2,128)S(1)} %get-tuple-element.36, f32[2,1024]{1,0:T(2,128)S(1)} %get-tuple-element.37), kind=kOutput, calls=%fused_computation.41 | convolution fusion | flops 1625817088 | bytes 2113536 | tf_op jit(solution)/shard_map/...n,nk->...k/dot_general | solution.py:34
  309.4 18.7 %fusion.4 = f32[32,2,1024]{2,0,1:T(8,128)S(1)} fusion(f32[1,32,2,1024]{3,1,2,0:T(8,128)S(1)} %get-tuple-element.23), kind=kOutput, calls=%fused_computation.7 | convolution fusion | flops 819986432 | bytes 524288 | tf_op jit(solution)/shard_map/...k,kn->...n/dot_general | solution.py:34
  328.1 18.2 %fusion.2 = f32[32,2,1024]{2,0,1:T(8,128)S(1)} fusion(f32[1,32,2,1024]{3,1,2,0:T(8,128)S(1)} %get-tuple-element.24), kind=kOutput, calls=%fused_computation.5 | convolution fusion | flops 819986432 | bytes 524288 | tf_op jit(solution)/shard_map/...k,kn->...n/dot_general | solution.py:34
  346.3 18.3 %fusion.48 = f32[32,2,1024]{2,0,1:T(8,128)S(1)} fusion(f32[32,2,1024]{2,0,1:T(8,128)S(1)} %fusion.4, f32[1,32,2,1024]{3,1,2,0:T(8,128)S(1)} %get-tuple-element.24), kind=kOutput, calls=%fused_computation.42 | convolution fusion | flops 820051968 | bytes 786432 | tf_op jit(solution)/shard_map/...k,kn->...n/dot_general | solution.py:34
  364.6 18.2 %multiply_add_fusion.1 = (f32[32,2,1024]{2,0,1:T(8,128)S(1)}, f32[32,2,1024]{2,0,1:T(8,128)S(1)}) fusion(f32[32,2,1024]{2,0,1:T(8,128)S(1)} %fusion.48, f32[2,1024]{1,0:T(2,128)S(1)} %get-tuple-element.35, f32[2,1024]{1,0:T(2,128)S(1)} %get-tuple-element.34, f32[32,2,1024]{2,0,1:T(8,128)S(1)} %fusion.2, f32[1,32,2,1024]{3,1,2,0:T(8,128)S(1)} %get-tuple-element.23), kind=kOutput, calls=%fused_computation.80 | convolution fusion | flops 820445184 | bytes 1327104 | tf_op jit(solution)/shard_map/...k,kn->...n/dot_general | solution.py:34
  384.3 5.0 collective-permute-done.12
  389.3 5.6 %collective-permute-done.11 = f32[32,2,1024]{2,0,1:T(8,128)S(1)} collective-permute-done((f32[32,2,1024]{2,0,1:T(8,128)S(1)}, f32[32,2,1024]{2,0,1:T(8,128)S(1)}, u32[]{:S(2)}, u32[]{:S(2)}) %collective-permute-start.11) | collective-permute-done | bytes 262176 | tf_op jit(solution)/shard_map/ppermute | solution.py:16
  397.7 17.4 %collective-permute-done.14 = f32[32,2,1024]{2,0,1:T(8,128)S(1)} collective-permute-done((f32[32,2,1024]{2,0,1:T(8,128)S(1)}, f32[32,2,1024]{2,0,1:T(8,128)S(1)}, u32[]{:S(2)}, u32[]{:S(2)}) %collective-permute-start.14) | collective-permute-done | bytes 262176 | tf_op jit(solution)/shard_map/ppermute | solution.py:16
  415.8 5.0 collective-permute-done.13
  427.8 17.2 %collective-permute-done.16 = f32[32,2,1024]{2,0,1:T(8,128)S(1)} collective-permute-done((f32[32,2,1024]{2,0,1:T(8,128)S(1)}, f32[32,2,1024]{2,0,1:T(8,128)S(1)}, u32[]{:S(2)}, u32[]{:S(2)}) %collective-permute-start.16) | collective-permute-done | bytes 262176 | tf_op jit(solution)/shard_map/ppermute | solution.py:16
  445.8 5.0 collective-permute-done.15
  453.7 5.8 %collective-permute-done.18 = f32[32,2,1024]{2,0,1:T(8,128)S(1)} collective-permute-done((f32[32,2,1024]{2,0,1:T(8,128)S(1)}, f32[32,2,1024]{2,0,1:T(8,128)S(1)}, u32[]{:S(2)}, u32[]{:S(2)}) %collective-permute-start.18) | collective-permute-done | bytes 262176 | tf_op jit(solution)/shard_map/ppermute | solution.py:16
  460.2 5.0 collective-permute-done.17
  469.6 4.8 collective-permute-done.19
  474.4 5.6 %collective-permute-done.20 = f32[32,2,1024]{2,0,1:T(8,128)S(1)} collective-permute-done((f32[32,2,1024]{2,0,1:T(8,128)S(1)}, f32[32,2,1024]{2,0,1:T(8,128)S(1)}, u32[]{:S(2)}, u32[]{:S(2)}) %collective-permute-start.20) | collective-permute-done | bytes 262176 | tf_op jit(solution)/shard_map/ppermute | solution.py:16
  480.3 27.1 %all_gather.3 = bf16[256,1024]{1,0:T(8,128)(2,1)S(1)} all-gather(bf16[32,1024]{1,0:T(8,128)(2,1)S(1)} %fusion.72), channel_id=1, replica_groups=mesh['ctx'=32,'ch'=8] {'ch'}, dimensions={0}, use_global_device_ids=true | all-gather | bytes 589824 | tf_op jit(solution)/shard_map/all_gather | solution.py:142
  (70 shorter events, 54.8 us)
Async XLA Ops:
  6.5 1.6 copy-start
  6.5 46.0 %reduce-scatter.2.cloned.1.call-start = ((), (), s32[]{:S(2)}) async-start(), calls=%async_computation.1 | async-start | bytes 3538944 | tf_op jit(solution)/shard_map/reduce_scatter | solution.py:114
  13.0 46.2 %copy-start.5 = (f32[32,1024]{1,0:T(8,128)S(1)}, f32[32,1024]{1,0:T(8,128)}, u32[]{:S(2)}) copy-start(f32[32,1024]{1,0:T(8,128)} %param.9) | copy-start | bytes 393220
  53.4 4.1 collective-permute-start
  60.2 13.0 %collective-permute-start.1 = (f32[2,32,2,1024]{3,1,2,0:T(8,128)}, f32[2,32,2,1024]{3,1,2,0:T(8,128)}, u32[]{:S(2)}, u32[]{:S(2)}) collective-permute-start(f32[2,32,2,1024]{3,1,2,0:T(8,128)} %pad_maximum_fusion), channel_id=1, source_target_pairs={{0,128},{8,136},{16,144},{24,152},{32,160},{40,168},{48,176},{56,1... | collective-permute-start | bytes 1572872 | tf_op jit(solution)/shard_map/ppermute | solution.py:16
  66.3 18.1 %collective-permute-start.2 = (f32[2,32,2,1024]{3,1,2,0:T(8,128)}, f32[2,32,2,1024]{3,1,2,0:T(8,128)}, u32[]{:S(2)}, u32[]{:S(2)}) collective-permute-start(f32[2,32,2,1024]{3,1,2,0:T(8,128)} %stack.31), channel_id=1, source_target_pairs={{0,128},{8,136},{16,144},{24,152},{32,160},{40,168},{48,176},{56,1... | collective-permute-start | bytes 1572872 | tf_op jit(solution)/shard_map/ppermute | solution.py:16
  86.8 8.2 %collective-permute-start.3 = (f32[2,32,2,1024]{3,1,2,0:T(8,128)}, f32[2,32,2,1024]{3,1,2,0:T(8,128)S(1)}, u32[]{:S(2)}, u32[]{:S(2)}) collective-permute-start(f32[2,32,2,1024]{3,1,2,0:T(8,128)} %get-tuple-element.13), channel_id=1, source_target_pairs={{0,64},{8,72},{16,80},{24,88},{32,96},{40,104},{48,112},{56,120},{... | collective-permute-start | bytes 1572872 | tf_op jit(solution)/shard_map/ppermute | solution.py:16
  88.1 18.2 %collective-permute-start.4 = (f32[2,32,2,1024]{3,1,2,0:T(8,128)}, f32[2,32,2,1024]{3,1,2,0:T(8,128)}, u32[]{:S(2)}, u32[]{:S(2)}) collective-permute-start(f32[2,32,2,1024]{3,1,2,0:T(8,128)} %get-tuple-element.14), channel_id=1, source_target_pairs={{0,64},{8,72},{16,80},{24,88},{32,96},{40,104},{48,112},{56,120},{... | collective-permute-start | bytes 1572872 | tf_op jit(solution)/shard_map/ppermute | solution.py:16
  95.1 0.8 copy-start.3
  108.0 34.5 %copy-start.1 = (f32[2,32,2,1024]{3,1,2,0:T(8,128)}, f32[2,32,2,1024]{3,1,2,0:T(8,128)S(1)}, u32[]{:S(2)}) copy-start(f32[2,32,2,1024]{3,1,2,0:T(8,128)S(1)} %get-tuple-element.11) | copy-start | bytes 1572868
  108.0 34.5 %copy-start.2 = (f32[2,32,2,1024]{3,1,2,0:T(8,128)}, f32[2,32,2,1024]{3,1,2,0:T(8,128)S(1)}, u32[]{:S(2)}) copy-start(f32[2,32,2,1024]{3,1,2,0:T(8,128)S(1)} %get-tuple-element.12) | copy-start | bytes 1572868
  108.0 34.5 %collective-permute-start.5 = (f32[2,32,2,1024]{3,1,2,0:T(8,128)S(1)}, f32[2,32,2,1024]{3,1,2,0:T(8,128)}, u32[]{:S(2)}, u32[]{:S(2)}) collective-permute-start(f32[2,32,2,1024]{3,1,2,0:T(8,128)S(1)} %get-tuple-element.11), channel_id=1, source_target_pairs={{0,32},{8,40},{16,48},{24,56},{32,0},{40,8},{48,16},{56,24},{64,96... | collective-permute-start | bytes 1572872 | tf_op jit(solution)/shard_map/ppermute | solution.py:16
  112.5 44.7 %collective-permute-start.6 = (f32[2,32,2,1024]{3,1,2,0:T(8,128)S(1)}, f32[2,32,2,1024]{3,1,2,0:T(8,128)}, u32[]{:S(2)}, u32[]{:S(2)}) collective-permute-start(f32[2,32,2,1024]{3,1,2,0:T(8,128)S(1)} %get-tuple-element.12), channel_id=1, source_target_pairs={{0,32},{8,40},{16,48},{24,56},{32,0},{40,8},{48,16},{56,24},{64,96... | collective-permute-start | bytes 1572872 | tf_op jit(solution)/shard_map/ppermute | solution.py:16
  158.9 37.0 %collective-permute-start.7 = (f32[2,32,2,1024]{3,1,2,0:T(8,128)S(1)}, f32[2,32,2,1024]{3,1,2,0:T(8,128)}, u32[]{:S(2)}, u32[]{:S(2)}) collective-permute-start(f32[2,32,2,1024]{3,1,2,0:T(8,128)S(1)} %get-tuple-element.9), channel_id=1, source_target_pairs={{0,16},{8,24},{16,0},{24,8},{32,48},{40,56},{48,32},{56,40},{64,80... | collective-permute-start | bytes 1572872 | tf_op jit(solution)/shard_map/ppermute | solution.py:16
  159.0 48.1 %collective-permute-start.8 = (f32[2,32,2,1024]{3,1,2,0:T(8,128)S(1)}, f32[2,32,2,1024]{3,1,2,0:T(8,128)}, u32[]{:S(2)}, u32[]{:S(2)}) collective-permute-start(f32[2,32,2,1024]{3,1,2,0:T(8,128)S(1)} %get-tuple-element.10), channel_id=1, source_target_pairs={{0,16},{8,24},{16,0},{24,8},{32,48},{40,56},{48,32},{56,40},{64,80... | collective-permute-start | bytes 1572872 | tf_op jit(solution)/shard_map/ppermute | solution.py:16
  209.5 13.2 %collective-permute-start.9 = (f32[2,32,2,1024]{3,1,2,0:T(8,128)}, f32[2,32,2,1024]{3,1,2,0:T(8,128)S(1)}, u32[]{:S(2)}, u32[]{:S(2)}) collective-permute-start(f32[2,32,2,1024]{3,1,2,0:T(8,128)} %get-tuple-element.7), channel_id=1, source_target_pairs={{0,8},{8,0},{16,24},{24,16},{32,40},{40,32},{48,56},{56,48},{64,72... | collective-permute-start | bytes 1572872 | tf_op jit(solution)/shard_map/ppermute | solution.py:16
  209.6 24.4 %collective-permute-start.10 = (f32[2,32,2,1024]{3,1,2,0:T(8,128)}, f32[2,32,2,1024]{3,1,2,0:T(8,128)S(1)}, u32[]{:S(2)}, u32[]{:S(2)}) collective-permute-start(f32[2,32,2,1024]{3,1,2,0:T(8,128)} %get-tuple-element.8), channel_id=1, source_target_pairs={{0,8},{8,0},{16,24},{24,16},{32,40},{40,32},{48,56},{56,48},{64,72... | collective-permute-start | bytes 1572872 | tf_op jit(solution)/shard_map/ppermute | solution.py:16
  382.8 6.5 %collective-permute-start.12 = (f32[32,2,1024]{2,0,1:T(8,128)S(1)}, f32[32,2,1024]{2,0,1:T(8,128)S(1)}, u32[]{:S(2)}, u32[]{:S(2)}) collective-permute-start(f32[32,2,1024]{2,0,1:T(8,128)S(1)} %get-tuple-element.25), channel_id=1, source_target_pairs={{0,8},{8,0},{16,24},{24,16},{32,40},{40,32},{48,56},{56,48},{64,72... | collective-permute-start | bytes 786440 | tf_op jit(solution)/shard_map/ppermute | solution.py:16
  383.2 11.8 %collective-permute-start.11 = (f32[32,2,1024]{2,0,1:T(8,128)S(1)}, f32[32,2,1024]{2,0,1:T(8,128)S(1)}, u32[]{:S(2)}, u32[]{:S(2)}) collective-permute-start(f32[32,2,1024]{2,0,1:T(8,128)S(1)} %get-tuple-element.26), channel_id=1, source_target_pairs={{0,8},{8,0},{16,24},{24,16},{32,40},{40,32},{48,56},{56,48},{64,72... | collective-permute-start | bytes 786440 | tf_op jit(solution)/shard_map/ppermute | solution.py:16
  395.0 85.1 %copy-start.10 = (f32[32]{0:T(128)S(1)}, f32[32]{0:T(128)}, u32[]{:S(2)}) copy-start(f32[32]{0:T(128)} %param.10) | copy-start | bytes 388
  395.1 20.0 %collective-permute-start.14 = (f32[32,2,1024]{2,0,1:T(8,128)S(1)}, f32[32,2,1024]{2,0,1:T(8,128)S(1)}, u32[]{:S(2)}, u32[]{:S(2)}) collective-permute-start(f32[32,2,1024]{2,0,1:T(8,128)S(1)} %get-tuple-element.21), channel_id=1, source_target_pairs={{0,16},{8,24},{16,0},{24,8},{32,48},{40,56},{48,32},{56,40},{64,80... | collective-permute-start | bytes 786440 | tf_op jit(solution)/shard_map/ppermute | solution.py:16
  396.0 24.9 %collective-permute-start.13 = (f32[32,2,1024]{2,0,1:T(8,128)S(1)}, f32[32,2,1024]{2,0,1:T(8,128)}, u32[]{:S(2)}, u32[]{:S(2)}) collective-permute-start(f32[32,2,1024]{2,0,1:T(8,128)S(1)} %get-tuple-element.22), channel_id=1, source_target_pairs={{0,16},{8,24},{16,0},{24,8},{32,48},{40,56},{48,32},{56,40},{64,80... | collective-permute-start | bytes 786440 | tf_op jit(solution)/shard_map/ppermute | solution.py:16
  415.1 0.7 copy-start.6
  422.0 23.1 %collective-permute-start.16 = (f32[32,2,1024]{2,0,1:T(8,128)S(1)}, f32[32,2,1024]{2,0,1:T(8,128)S(1)}, u32[]{:S(2)}, u32[]{:S(2)}) collective-permute-start(f32[32,2,1024]{2,0,1:T(8,128)S(1)} %get-tuple-element.19), channel_id=1, source_target_pairs={{0,32},{8,40},{16,48},{24,56},{32,0},{40,8},{48,16},{56,24},{64,96... | collective-permute-start | bytes 786440 | tf_op jit(solution)/shard_map/ppermute | solution.py:16
  424.9 25.9 %collective-permute-start.15 = (f32[32,2,1024]{2,0,1:T(8,128)S(1)}, f32[32,2,1024]{2,0,1:T(8,128)}, u32[]{:S(2)}, u32[]{:S(2)}) collective-permute-start(f32[32,2,1024]{2,0,1:T(8,128)S(1)} %get-tuple-element.20), channel_id=1, source_target_pairs={{0,32},{8,40},{16,48},{24,56},{32,0},{40,8},{48,16},{56,24},{64,96... | collective-permute-start | bytes 786440 | tf_op jit(solution)/shard_map/ppermute | solution.py:16
  445.1 0.7 copy-start.7
  452.0 7.5 %collective-permute-start.18 = (f32[32,2,1024]{2,0,1:T(8,128)S(1)}, f32[32,2,1024]{2,0,1:T(8,128)S(1)}, u32[]{:S(2)}, u32[]{:S(2)}) collective-permute-start(f32[32,2,1024]{2,0,1:T(8,128)S(1)} %get-tuple-element.17), channel_id=1, source_target_pairs={{0,64},{8,72},{16,80},{24,88},{32,96},{40,104},{48,112},{56,120},{... | collective-permute-start | bytes 786440 | tf_op jit(solution)/shard_map/ppermute | solution.py:16
  452.6 12.5 %collective-permute-start.17 = (f32[32,2,1024]{2,0,1:T(8,128)S(1)}, f32[32,2,1024]{2,0,1:T(8,128)}, u32[]{:S(2)}, u32[]{:S(2)}) collective-permute-start(f32[32,2,1024]{2,0,1:T(8,128)S(1)} %get-tuple-element.18), channel_id=1, source_target_pairs={{0,64},{8,72},{16,80},{24,88},{32,96},{40,104},{48,112},{56,120},{... | collective-permute-start | bytes 786440 | tf_op jit(solution)/shard_map/ppermute | solution.py:16
  459.5 0.7 copy-start.8
  466.4 8.1 %collective-permute-start.19 = (f32[32,2,1024]{2,0,1:T(8,128)S(1)}, f32[32,2,1024]{2,0,1:T(8,128)S(1)}, u32[]{:S(2)}, u32[]{:S(2)}) collective-permute-start(f32[32,2,1024]{2,0,1:T(8,128)S(1)} %get-tuple-element.16), channel_id=1, source_target_pairs={{0,128},{8,136},{16,144},{24,152},{32,160},{40,168},{48,176},{56,1... | collective-permute-start | bytes 786440 | tf_op jit(solution)/shard_map/ppermute | solution.py:16
  469.0 11.1 %collective-permute-start.20 = (f32[32,2,1024]{2,0,1:T(8,128)S(1)}, f32[32,2,1024]{2,0,1:T(8,128)S(1)}, u32[]{:S(2)}, u32[]{:S(2)}) collective-permute-start(f32[32,2,1024]{2,0,1:T(8,128)S(1)} %get-tuple-element.15), channel_id=1, source_target_pairs={{0,128},{8,136},{16,144},{24,152},{32,160},{40,168},{48,176},{56,1... | collective-permute-start | bytes 786440 | tf_op jit(solution)/shard_map/ppermute | solution.py:16
  469.6 37.8 %copy-start.4 = (bf16[256,1024]{1,0:T(8,128)(2,1)S(1)}, bf16[256,1024]{1,0:T(8,128)(2,1)}, u32[]{:S(2)}) copy-start(bf16[256,1024]{1,0:T(8,128)(2,1)} %param.11) | copy-start | bytes 1572868
  (1 other events, 0.7 us)
Sparse Core Ops, SparseCore 0:
  13.2 39.3 reduce-scatter.1
where the time goes:
time: 524 us; the launch traced here: 516 us
  waiting for transfers between devices  263 us (50%)
  matrix products  154 us (29%)
  starting transfers between devices  33.5 us (6%)
  blocking collectives  27.1 us (5%)
  other arithmetic  16.6 us (3%)
  between operations  15.3 us (3%)
  local copies, waits for them, and re-layouts  6.93 us (1%)
    ppermute x20, waiting for transfers between devices, from_partner(): lax.ppermute(value, axis, [(i, i ^ 1 << stride) for i in range(lax.axis_s...  223 us
    dot_general x8, matrix products, multiply(): return jnp.einsum(pattern, left, table, precision=HIGHEST)  147 us
    reduce_scatter x1, waiting for transfers between devices, per_device(): lax.psum_scatter(jnp.einsum('td,jdc->cjt', tokens, in_proj, preferred_ele...  38.8 us
    ppermute x20, starting transfers between devices, from_partner(): lax.ppermute(value, axis, [(i, i ^ 1 << stride) for i in range(lax.axis_s...  30.6 us
    all_gather x1, blocking collectives, per_device(): lax.all_gather(gated, 'ch', axis=0, tiled=True)  27.1 us
  transfers between devices with their start and end apart: 22, of which 22 were waited for; matrix products, arithmetic and copies ran while one was open for 0% of the time, Pallas kernels for 0%

commit v1 on v0

v1 whole, which is shorter than its diff:
```python
import functools

import jax
import jax.numpy as jnp
import ml_dtypes
import numpy as np
from jax import lax
from jax.experimental import pallas as pl
from jax.experimental.pallas import tpu as pltpu
from jax.sharding import PartitionSpec as P

MESH = pl.DeviceIdType.MESH
BF = jnp.bfloat16
F32 = jnp.float32
NCTX = 32
NY = 4
CH = 32
TOK = 1024
HALF = 512
ROWS = 256
LANE = 128


def split_np(table):
    high = table.astype(ml_dtypes.bfloat16)
    low = (table - high.astype(np.float64)).astype(ml_dtypes.bfloat16)
    return high, low


def tables():
    n1 = np.arange(256)
    k1 = np.arange(256) + 0.5
    angle = 2 * np.pi * np.outer(k1, n1) / 512
    first = np.concatenate([np.cos(angle), -np.sin(angle)], axis=0)
    last = first.T
    n2 = np.arange(128)
    angle = 2 * np.pi * np.outer(n2, n2) / 128
    c, s = np.cos(angle), np.sin(angle)
    forward = np.block([[c, -s], [s, c]])
    backward = np.block([[c, s], [-s, c]])
    angle = 2 * np.pi * np.outer(k1, n2) / 65536
    twist = np.stack([np.cos(angle), -np.sin(angle)]).astype(np.float32)
    return (
        np.stack(split_np(first)),
        np.stack(split_np(last)),
        np.stack(split_np(forward) + split_np(backward)),
        twist,
    )


def dot(a, b, dims=((1,), (0,))):
    return lax.dot_general(a, b, (dims, ((), ())), preferred_element_type=F32)


def split(value):
    high = value.astype(BF)
    return high, (value - high.astype(F32)).astype(BF)


def forward_transform(x, first, mid, twist):
    high, low = split(x)
    both = dot(first[0], jnp.concatenate([high, low], axis=1))
    a = both[:, :LANE] + both[:, LANE:] + dot(first[1], high)
    re, im = a[:ROWS], a[ROWS:]
    cos, sin = twist[0], twist[1]
    turned = jnp.concatenate([re * cos - im * sin, re * sin + im * cos], axis=1)
    high, low = split(turned)
    return dot(high, mid[0]) + (dot(low, mid[0]) + dot(high, mid[1]))


def inverse_transform(re, im, last, mid, twist):
    high, low = split(jnp.concatenate([re, im], axis=1))
    z = dot(high, mid[2]) + (dot(low, mid[2]) + dot(high, mid[3]))
    re, im = z[:, :LANE], z[:, LANE:]
    cos, sin = twist[0], twist[1]
    turned = jnp.concatenate([re * cos + im * sin, im * cos - re * sin], axis=0)
    high, low = split(turned)
    both = dot(last[0], jnp.concatenate([high, low], axis=1))
    return both[:, :LANE] + both[:, LANE:] + dot(last[1], high)


def rows_of(index):
    return pl.ds(pl.multiple_of(index * 8, 8), 8)


def kernel(
    tok_hbm, w_hbm, taps, filt_hbm, skip, first_hbm, last_hbm, mid_hbm, twist_hbm, out_ref,
    tok, w, wt, filt, first, last, mid, twist,
    part, from_core, y_send, y_recv, part0, from_core0, y_send0, y_recv0,
    proj, halo, halo0, cols, carried, car_rows, filt_rows, x_rows, h_rows, spec, y_rows, back_rows, feat0,
    load_sem, core_send, core_recv, ys_sem, yr_sem, halo_send, halo_recv, a2a_send, a2a_recv, g_send, g_recv,
):
    ctx = lax.axis_index("ctx")
    ch = lax.axis_index("ch")
    y = ch // 2
    core = ch % 2

    def at_y(step):
        return {"ctx": ctx, "ch": lax.rem(y + step, NY) * 2 + core}

    partner = {"ctx": ctx, "ch": y * 2 + 1 - core}

    def at_ctx(index):
        return {"ctx": index, "ch": ch}

    def remote(src, dst, send, recv, device):
        return pltpu.make_async_remote_copy(
            src_ref=src, dst_ref=dst, send_sem=send, recv_sem=recv, device_id=device, device_id_type=MESH
        )

    loads = [
        (w_hbm.at[1], w.at[1]),
        (tok_hbm.at[pl.ds(HALF, HALF)], tok.at[pl.ds(HALF, HALF)]),
        (w_hbm.at[2], w.at[2]),
        (tok_hbm.at[pl.ds(0, HALF)], tok.at[pl.ds(0, HALF)]),
        (w_hbm.at[0], w.at[0]),
        (filt_hbm, filt),
        (first_hbm, first),
        (mid_hbm, mid),
        (twist_hbm, twist),
        (last_hbm, last),
    ]
    loads = [pltpu.make_async_copy(src, dst, load_sem.at[n]) for n, (src, dst) in enumerate(loads)]
    for load in loads:
        load.start()

    barrier = pltpu.get_barrier_semaphore()

    def greet(step, carry):
        pl.semaphore_signal(barrier, inc=1, device_id=at_ctx(lax.rem(ctx + step, NCTX)), device_id_type=MESH)
        return carry

    lax.fori_loop(1, NCTX, greet, 0)
    for step in range(1, NY):
        pl.semaphore_signal(barrier, inc=1, device_id=at_y(step), device_id_type=MESH)
    pl.semaphore_signal(barrier, inc=1, device_id=partner, device_id_type=MESH)

    eye = (
        lax.broadcasted_iota(jnp.int32, (256, 256), 0) == lax.broadcasted_iota(jnp.int32, (256, 256), 1)
    ).astype(F32).astype(BF)

    def transpose_weights(j):
        for block in range(4):
            rows = pl.ds(block * 256, 256)
            wt[j, :, rows] = dot(eye, w[j, rows, :], ((1,), (1,))).astype(BF)

    def project(j, q):
        return dot(wt[j], tok[pl.ds(q * HALF, HALF), :], ((1,), (1,)))

    def project_inner(q):
        for j in (1, 2):
            if q == 1:
                loads[0 if j == 1 else 2].wait()
                transpose_weights(j)
                if j == 1:
                    loads[1].wait()
            value = project(j, q)
            for k in range(8):
                part[q, k % 2, k // 2, j - 1] = value[k * CH:(k + 1) * CH]

    def core_copy(q):
        return remote(part.at[q, 1 - core], from_core.at[q], core_send.at[q], core_recv.at[q], partner)

    def y_copy(q, step):
        return remote(y_send.at[q, step - 1], y_recv.at[q, step - 1], ys_sem.at[q, step - 1], yr_sem.at[q, step - 1],
                      at_y(step))

    def y_copy0(step):
        return remote(y_send0.at[step - 1], y_recv0.at[step - 1], ys_sem.at[2, step - 1], yr_sem.at[2, step - 1],
                      at_y(step))

    project_inner(1)
    pl.semaphore_wait(barrier, NCTX + NY - 1)
    core_copy(1).start()
    loads[3].wait()
    project_inner(0)
    core_copy(0).start()

    for q in (1, 0):
        core_copy(q).wait_recv()
        for step in range(1, NY):
            to = lax.rem(y + step, NY)
            y_send[q, step - 1] = (part[q, core, to] + from_core[q, to]).astype(BF)
            y_copy(q, step).start()

    loads[4].wait()
    transpose_weights(0)
    for q in (1, 0):
        value = project(0, q)
        for k in range(8):
            part0[k % 2, k // 2, :, pl.ds(q * HALF, HALF)] = value[k * CH:(k + 1) * CH]
    core_copy0 = remote(part0.at[1 - core], from_core0, core_send.at[2], core_recv.at[2], partner)
    core_copy0.start()

    def exchange(src, dst, slot):
        def send(step, carry):
            peer = lax.rem(ctx + step, NCTX)
            remote(src.at[rows_of(peer)], dst.at[rows_of(ctx)], a2a_send.at[slot], a2a_recv.at[slot],
                   at_ctx(peer)).start()
            return carry

        lax.fori_loop(1, NCTX, send, 0)
        dst[rows_of(ctx), :] = src[rows_of(ctx), :]

    def all_of(src, dst, slot):
        others = pl.ds(0, ROWS - 8)
        return remote(src.at[others], dst.at[others], a2a_send.at[slot], a2a_recv.at[slot],
                      at_ctx(lax.rem(ctx + 1, NCTX)))

    def to_rows(value, dst):
        for g in range(CH // 8):
            for a in range(8):
                dst[pl.ds(64 * g + a, 8, stride=8), :] = value[8 * g:8 * g + 8, LANE * a:LANE * a + LANE]

    loads[5].wait()
    to_rows(filt[...], filt_rows)
    exchange(filt_rows, h_rows, 0)

    core_copy0.wait_recv()
    for step in range(1, NY):
        to = lax.rem(y + step, NY)
        y_send0[step - 1] = part0[core, to] + from_core0[to]
        y_copy0(step).start()

    sublane = lax.broadcasted_iota(jnp.int32, (8, LANE), 0)

    def column(read, slot):
        for g in range(CH // 8):
            value = jnp.full((8, LANE), read(8 * g), F32)
            for r in range(1, 8):
                value = jnp.where(sublane == r, read(8 * g + r), value)
            cols[slot, pl.ds(8 * g, 8), :] = value

    for j in range(3):
        for lag in range(3):
            column(lambda c, j=j, lag=lag: taps[j, lag, c], 3 * j + lag)
    column(lambda c: skip[c], 9)

    def finish_inner(q):
        for step in range(1, NY):
            y_copy(q, step).wait_recv()
        total = part[q, core, y] + from_core[q, y]
        for step in range(1, NY):
            total = total + y_recv[q, step - 1].astype(F32)
        proj[pl.ds(1, 2), :, pl.ds(q * HALF, HALF)] = total

    after = at_ctx(lax.rem(ctx + 1, NCTX))
    finish_inner(1)
    halo_copy = remote(proj.at[pl.ds(1, 2), :, pl.ds(TOK - LANE, LANE)], halo, halo_send.at[0], halo_recv.at[0], after)
    halo_copy.start()

    for n in (6, 7, 8):
        loads[n].wait()
    h_copies = all_of(filt_rows, h_rows, 0)
    h_copies.wait_recv()
    spec[...] = forward_transform(h_rows[...], first, mid, twist) * (2.0 / 65536)

    finish_inner(0)
    halo_copy.wait_recv()
    has_past = (ctx > 0).astype(F32)

    def featured(j, past):
        extended = jnp.concatenate([past * has_past, proj[j]], axis=1)
        total = jnp.zeros((CH, TOK), F32)
        for lag in range(3):
            moved = extended if lag == 0 else pltpu.roll(extended, lag, 1)
            tap = jnp.concatenate([cols[3 * j + lag]] * (TOK // LANE), axis=1)
            total = total + tap * moved[:, LANE:]
        return total

    carried[...] = featured(1, halo[0]) * featured(2, halo[1])
    to_rows(carried[...], car_rows)
    exchange(car_rows, x_rows, 1)

    for step in range(1, NY):
        y_copy0(step).wait_recv()
    total0 = part0[core, y] + from_core0[y]
    for step in range(1, NY):
        total0 = total0 + y_recv0[step - 1]
    proj[0] = total0
    halo_copy0 = remote(proj.at[0, :, pl.ds(TOK - LANE, LANE)], halo0, halo_send.at[1], halo_recv.at[1], after)
    halo_copy0.start()

    loads[9].wait()
    x_copies = all_of(car_rows, x_rows, 1)
    x_copies.wait_recv()
    x_spec = forward_transform(x_rows[...], first, mid, twist)
    xr, xi = x_spec[:, :LANE], x_spec[:, LANE:]
    hr, hi = spec[:, pl.ds(0, LANE)], spec[:, pl.ds(LANE, LANE)]
    y_rows[...] = inverse_transform(xr * hr - xi * hi, xr * hi + xi * hr, last, mid, twist)
    exchange(y_rows, back_rows, 2)

    halo_copy0.wait_recv()
    feat0[...] = featured(0, halo0[...])
    y_copies = all_of(y_rows, back_rows, 2)
    y_copies.wait_recv()
    for g in range(CH // 8):
        for a in range(8):
            rows, lanes = pl.ds(8 * g, 8), pl.ds(LANE * a, LANE)
            conv = back_rows[pl.ds(64 * g + a, 8, stride=8), :]
            feat0[rows, lanes] = feat0[rows, lanes] * (conv + cols[9, rows, :] * carried[rows, lanes])
    out_ref[ch] = feat0[...].astype(BF)

    def gather(slot, send, device):
        return remote(out_ref.at[slot], out_ref.at[slot], g_send.at[send], g_recv.at[send], device)

    sends = [gather(ch, step - 1, at_y(step)) for step in range(1, NY)]
    sends.append(gather(ch, 3, partner))
    for copy in sends:
        copy.start()
    for step in range(1, NY):
        came = lax.rem(y + NY - step, NY) * 2 + core
        gather(came, step - 1, at_y(step)).wait_recv()
        passed = gather(came, 3 + step, partner)
        passed.start()
        sends.append(passed)
    for send in range(3, 7):
        gather(ch, send, partner).wait_recv()

    for copy in sends:
        copy.wait_send()
    for q in range(2):
        core_copy(q).wait_send()
        for step in range(1, NY):
            y_copy(q, step).wait_send()
    core_copy0.wait_send()
    for step in range(1, NY):
        y_copy0(step).wait_send()
    for copy in (halo_copy, halo_copy0, h_copies, x_copies, y_copies):
        copy.wait_send()


def gated_values(tokens, in_proj, short_taps, long_filter, skip_gain):
    first, last, mid, twist = (jnp.asarray(t) for t in tables())
    hbm = pl.BlockSpec(memory_space=pltpu.HBM)
    smem = pl.BlockSpec(memory_space=pltpu.SMEM)
    vmem = pltpu.VMEM
    dma = pltpu.SemaphoreType.DMA
    scratch = [
        vmem((TOK, 1024), BF), vmem((3, 1024, 256), BF), vmem((3, 256, 1024), BF), vmem((CH, TOK), F32),
        vmem(first.shape, BF), vmem(last.shape, BF), vmem(mid.shape, BF), vmem(twist.shape, F32),
        vmem((2, 2, NY, 2, CH, HALF), F32), vmem((2, NY, 2, CH, HALF), F32),
        vmem((2, NY - 1, 2, CH, HALF), BF), vmem((2, NY - 1, 2, CH, HALF), BF),
        vmem((2, NY, CH, TOK), F32), vmem((NY, CH, TOK), F32),
        vmem((NY - 1, CH, TOK), F32), vmem((NY - 1, CH, TOK), F32),
        vmem((3, CH, TOK), F32), vmem((2, CH, LANE), F32), vmem((CH, LANE), F32), vmem((10, CH, LANE), F32),
        vmem((CH, TOK), F32), vmem((ROWS, LANE), F32), vmem((ROWS, LANE), F32), vmem((ROWS, LANE), F32),
        vmem((ROWS, LANE), F32), vmem((ROWS, 2 * LANE), F32), vmem((ROWS, LANE), F32), vmem((ROWS, LANE), F32),
        vmem((CH, TOK), F32),
        dma((10,)), dma((3,)), dma((3,)), dma((3, 3)), dma((3, 3)), dma((2,)), dma((2,)), dma((3,)), dma((3,)),
        dma((7,)), dma((7,)),
    ]
    return pl.pallas_call(
        kernel,
        out_shape=jax.ShapeDtypeStruct((8, CH, TOK), BF),
        in_specs=[hbm, hbm, smem, hbm, smem, hbm, hbm, hbm, hbm],
        out_specs=pl.BlockSpec(memory_space=pltpu.VMEM),
        scratch_shapes=scratch,
        compiler_params=pltpu.CompilerParams(
            collective_id=0, has_side_effects=True, vmem_limit_bytes=63 << 20
        ),
        name="hyena",
    )(tokens, in_proj, jnp.transpose(short_taps, (1, 2, 0)), long_filter, skip_gain, first, last, mid, twist)


def per_device(tokens, in_proj, short_taps, long_filter, skip_gain, out_proj):
    gated = gated_values(tokens, in_proj, short_taps, long_filter, skip_gain).reshape(8 * CH, TOK)
    return jnp.einsum("ct,cd->td", gated, out_proj, preferred_element_type=F32).astype(BF)


def solution(mesh):
    placed = (
        P("ctx", "ch"),
        P(None, "ch", None),
        P("ch", None, None),
        P("ch", "ctx"),
        P("ch"),
        P(None, "ch"),
    )
    return jax.shard_map(
        per_device, mesh=mesh, in_specs=placed, out_specs=P("ctx", "ch"), check_vma=False
    )
```

time: 524 us -> 48.9 us (0.09); the launches traced: 516 us -> 48.8 us
  waiting for transfers between devices: 263 us -> 0 us
  matrix products: 154 us -> 3.11 us
  Pallas kernels: 0 us -> 45.6 us
  starting transfers between devices: 33.5 us -> 0 us
  blocking collectives: 27.1 us -> 0 us
  other arithmetic: 16.6 us -> 0 us
  between operations: 15.3 us -> 0.02 us
  local copies, waits for them, and re-layouts: 6.93 us -> 0.01 us
    ppermute x21 -> x0, waiting for transfers between devices: 224 us -> none  [the longest x20 223 us: from_partner(): lax.ppermute(value, axis, [(i, i ^ 1 << stride) for i in range(lax.axis_s...]
    dot_general x10 -> x1, matrix products: 154 us -> 3.11 us  [per_device(): jnp.einsum('ct,cd->td', gated, out_proj, preferred_element_type=F32)]
    pallas_call x0 -> x1, Pallas kernels: none -> 45.6 us  [gated_values(): pl.pallas_call(kernel, out_shape=jax.ShapeDtypeStruct((8, CH, TOK), BF),...]
    reduce_scatter x1 -> x0, waiting for transfers between devices: 38.8 us -> none  [per_device(): lax.psum_scatter(jnp.einsum('td,jdc->cjt', tokens, in_proj, preferred_ele...]
    ppermute x21 -> x0, starting transfers between devices: 33.5 us -> none  [the longest x20 30.6 us: from_partner(): lax.ppermute(value, axis, [(i, i ^ 1 << stride) for i in range(lax.axis_s...]
    all_gather x1 -> x0, blocking collectives: 27.1 us -> none  [per_device(): lax.all_gather(gated, 'ch', axis=0, tiled=True)]
    select_n x10 -> x0, other arithmetic: 13.5 us -> none  [the longest x5 9.74 us: forward_butterfly(): real_part = jnp.where(upper, real_part + other_re, lower_re)]
  transfers between devices with their start and end apart: 22 -> 0, of which waited for: 22 -> 0; matrix products, arithmetic and copies ran while one was open for 0% -> 0% of each run, Pallas kernels for 0% -> 0%
where the time goes in v1:
time: 48.9 us; the launch traced here: 48.8 us
  Pallas kernels  45.6 us (93%)
  matrix products  3.11 us (6%)
    pallas_call x1, Pallas kernels, gated_values(): pl.pallas_call(kernel, out_shape=jax.ShapeDtypeStruct((8, CH, TOK), BF),...  45.6 us
    dot_general x1, matrix products, per_device(): jnp.einsum('ct,cd->td', gated, out_proj, preferred_element_type=F32)  3.11 us

profile of v1, /device:TPU:1, one launch (start us, length us, event | category | flops | bytes accessed | tf_op | source)
XLA Modules:
  0.0 48.8 jit_solution(4963272597631579528)
XLA Ops:
  0.0 0.0 copy-start
  0.0 45.6 %hyena.1 = bf16[8,32,1024]{2,1,0:T(8,128)(2,1)} custom-call(bf16[1024,1024]{1,0:T(8,128)(2,1)} %tok_hbm.1, bf16[3,1024,256]{2,1,0:T(8,128)(2,1)} %w_hbm.1, f32[3,3,32]{2,1,0:T(4,128)} %bitcast.5, f32[32,1024]{1,0:T(8,128)} %filt_hbm.1, f32[32]{0:T(128)} %skip.1, bf16[2,512,256]{2,1,0:T(8,128)(2,1)} %constant.8.clone.first_hbm, ...), custom_call_target="tpu_custom_call" | custom-call | tf_op jit(solution)/shard_map/hyena/pallas_call | solution.py:353
  45.7 0.0 copy-done
  45.7 3.1 %convolution_convert_fusion = bf16[1024,1024]{1,0:T(8,128)(2,1)} fusion(bf16[256,1024]{1,0:T(8,128)(2,1)} %bitcast.4, bf16[256,1024]{1,0:T(8,128)(2,1)S(1)} %copy-done), kind=kOutput, calls=%fused_computation | convolution fusion | flops 537919488 | bytes 3145728 | tf_op jit(solution)/shard_map/ct,cd->td/dot_general | solution.py:368
Async XLA Ops:
  0.0 45.7 %copy-start = (bf16[256,1024]{1,0:T(8,128)(2,1)S(1)}, bf16[256,1024]{1,0:T(8,128)(2,1)}, u32[]{:S(2)}) copy-start(bf16[256,1024]{1,0:T(8,128)(2,1)} %param.15) | copy-start | bytes 1572868

commit v2 on v1

--- a/solution.py
+++ b/solution.py
@@ -13,10 +13,14 @@
 BF = jnp.bfloat16
 F32 = jnp.float32
 NCTX = 32
-NY = 4
+NX, NY, NZ = 4, 4, 8
 CH = 32
 TOK = 1024
-HALF = 512
+PARTS = 4
+PART = TOK // PARTS
+HALF = TOK // 2
+PIECES = 1
+PIECE = TOK // PIECES
 ROWS = 256
 LANE = 128
 
@@ -88,7 +92,7 @@
     tok, w, wt, filt, first, last, mid, twist,
     part, from_core, y_send, y_recv, part0, from_core0, y_send0, y_recv0,
     proj, halo, halo0, cols, carried, car_rows, filt_rows, x_rows, h_rows, spec, y_rows, back_rows, feat0,
-    load_sem, core_send, core_recv, ys_sem, yr_sem, halo_send, halo_recv, a2a_send, a2a_recv, g_send, g_recv,
+    load_sem, core_send, core_recv, ys_sem, yr_sem, halo_send, halo_recv, a2a_send, a2a_recv, g_send, g_recv, ring_sem,
 ):
     ctx = lax.axis_index("ctx")
     ch = lax.axis_index("ch")
@@ -108,32 +112,52 @@
             src_ref=src, dst_ref=dst, send_sem=send, recv_sem=recv, device_id=device, device_id_type=MESH
         )
 
-    loads = [
-        (w_hbm.at[1], w.at[1]),
-        (tok_hbm.at[pl.ds(HALF, HALF)], tok.at[pl.ds(HALF, HALF)]),
-        (w_hbm.at[2], w.at[2]),
-        (tok_hbm.at[pl.ds(0, HALF)], tok.at[pl.ds(0, HALF)]),
+    order = tuple(reversed(range(PARTS)))
+    loads = [(w_hbm.at[1], w.at[1]), (w_hbm.at[2], w.at[2])]
+    loads += [(tok_hbm.at[pl.ds(q * PART, PART)], tok.at[pl.ds(q * PART, PART)]) for q in order]
+    loads += [
+        (filt_hbm, filt),
         (w_hbm.at[0], w.at[0]),
-        (filt_hbm, filt),
         (first_hbm, first),
         (mid_hbm, mid),
         (twist_hbm, twist),
         (last_hbm, last),
     ]
     loads = [pltpu.make_async_copy(src, dst, load_sem.at[n]) for n, (src, dst) in enumerate(loads)]
-    for load in loads:
+    late = 2 + PARTS
+    for load in loads[:late + 1]:
         load.start()
 
     barrier = pltpu.get_barrier_semaphore()
-
-    def greet(step, carry):
-        pl.semaphore_signal(barrier, inc=1, device_id=at_ctx(lax.rem(ctx + step, NCTX)), device_id_type=MESH)
-        return carry
-
-    lax.fori_loop(1, NCTX, greet, 0)
-    for step in range(1, NY):
-        pl.semaphore_signal(barrier, inc=1, device_id=at_y(step), device_id_type=MESH)
-    pl.semaphore_signal(barrier, inc=1, device_id=partner, device_id_type=MESH)
+    x_at = [lax.rem(ctx // NZ + d, NX) for d in range(NX)]
+    z_at = [lax.rem(ctx % NZ + d, NZ) for d in range(NZ)]
+
+    def signal(sem, device):
+        pl.semaphore_signal(sem, inc=1, device_id=device, device_id_type=MESH)
+
+    def along_x(step):
+        return at_ctx(x_at[step] * NZ + z_at[0])
+
+    def along_z(step):
+        return at_ctx(x_at[0] * NZ + z_at[step])
+
+    near = [at_y(2), at_y(1), at_y(3), along_z(2), along_z(6), along_x(2), along_z(1), along_z(7), along_x(1), along_x(3)]
+    after, before = at_ctx(lax.rem(ctx + 1, NCTX)), at_ctx(lax.rem(ctx + NCTX - 1, NCTX))
+    near += [partner, after, before]
+    for device in near:
+        signal(barrier, device)
+
+    def greet_ring():
+        signal(ring_sem.at[0], along_z(2))
+        signal(ring_sem.at[0], along_z(6))
+
+    def greet_plane():
+        pl.semaphore_wait(ring_sem.at[0], 2)
+        for step in (2, 1, 3):
+            signal(ring_sem.at[1], along_x(step))
+
+    def wait_plane():
+        pl.semaphore_wait(ring_sem.at[1], 3)
 
     eye = (
         lax.broadcasted_iota(jnp.int32, (256, 256), 0) == lax.broadcasted_iota(jnp.int32, (256, 256), 1)
@@ -144,17 +168,12 @@
             rows = pl.ds(block * 256, 256)
             wt[j, :, rows] = dot(eye, w[j, rows, :], ((1,), (1,))).astype(BF)
 
-    def project(j, q):
-        return dot(wt[j], tok[pl.ds(q * HALF, HALF), :], ((1,), (1,)))
+    def project(j, start, size):
+        return dot(wt[j], tok[pl.ds(start, size), :], ((1,), (1,)))
 
     def project_inner(q):
         for j in (1, 2):
-            if q == 1:
-                loads[0 if j == 1 else 2].wait()
-                transpose_weights(j)
-                if j == 1:
-                    loads[1].wait()
-            value = project(j, q)
+            value = project(j, q * PART, PART)
             for k in range(8):
                 part[q, k % 2, k // 2, j - 1] = value[k * CH:(k + 1) * CH]
 
@@ -166,40 +185,19 @@
                       at_y(step))
 
     def y_copy0(step):
-        return remote(y_send0.at[step - 1], y_recv0.at[step - 1], ys_sem.at[2, step - 1], yr_sem.at[2, step - 1],
+        return remote(y_send0.at[step - 1], y_recv0.at[step - 1], ys_sem.at[PARTS, step - 1], yr_sem.at[PARTS, step - 1],
                       at_y(step))
 
-    project_inner(1)
-    pl.semaphore_wait(barrier, NCTX + NY - 1)
-    core_copy(1).start()
-    loads[3].wait()
-    project_inner(0)
-    core_copy(0).start()
-
-    for q in (1, 0):
-        core_copy(q).wait_recv()
-        for step in range(1, NY):
-            to = lax.rem(y + step, NY)
-            y_send[q, step - 1] = (part[q, core, to] + from_core[q, to]).astype(BF)
-            y_copy(q, step).start()
-
-    loads[4].wait()
-    transpose_weights(0)
-    for q in (1, 0):
-        value = project(0, q)
-        for k in range(8):
-            part0[k % 2, k // 2, :, pl.ds(q * HALF, HALF)] = value[k * CH:(k + 1) * CH]
-    core_copy0 = remote(part0.at[1 - core], from_core0, core_send.at[2], core_recv.at[2], partner)
-    core_copy0.start()
+    def hops(place):
+        return min(place[0], NX - place[0]) + min(place[1], NZ - place[1])
+
+    far_first = sorted(((dx, dz) for dx in range(NX) for dz in range(NZ) if dx or dz), key=hops, reverse=True)
 
     def exchange(src, dst, slot):
-        def send(step, carry):
-            peer = lax.rem(ctx + step, NCTX)
+        for dx, dz in far_first:
+            peer = x_at[dx] * NZ + z_at[dz]
             remote(src.at[rows_of(peer)], dst.at[rows_of(ctx)], a2a_send.at[slot], a2a_recv.at[slot],
                    at_ctx(peer)).start()
-            return carry
-
-        lax.fori_loop(1, NCTX, send, 0)
         dst[rows_of(ctx), :] = src[rows_of(ctx), :]
 
     def all_of(src, dst, slot):
@@ -212,15 +210,41 @@
             for a in range(8):
                 dst[pl.ds(64 * g + a, 8, stride=8), :] = value[8 * g:8 * g + 8, LANE * a:LANE * a + LANE]
 
-    loads[5].wait()
+    def send_chip_sums(q):
+        core_copy(q).wait_recv()
+        for step in (2, 1, 3):
+            to = lax.rem(y + step, NY)
+            y_send[q, step - 1] = (part[q, core, to] + from_core[q, to]).astype(BF)
+            y_copy(q, step).start()
+
+    for n, j in enumerate((1, 2)):
+        loads[n].wait()
+        transpose_weights(j)
+    for n, q in enumerate(order):
+        loads[2 + n].wait()
+        project_inner(q)
+        if n == 0:
+            for load in loads[late + 1:]:
+                load.start()
+            pl.semaphore_wait(barrier, len(near))
+            greet_ring()
+        core_copy(q).start()
+        if n > 0:
+            send_chip_sums(order[n - 1])
+    send_chip_sums(order[-1])
+    greet_plane()
+
+    loads[late + 1].wait()
+    transpose_weights(0)
+    for q in range(2):
+        value = project(0, q * HALF, HALF)
+        for k in range(8):
+            part0[k % 2, k // 2, :, pl.ds(q * HALF, HALF)] = value[k * CH:(k + 1) * CH]
+    core_copy0 = remote(part0.at[1 - core], from_core0, core_send.at[PARTS], core_recv.at[PARTS], partner)
+    core_copy0.start()
+
+    loads[late].wait()
     to_rows(filt[...], filt_rows)
-    exchange(filt_rows, h_rows, 0)
-
-    core_copy0.wait_recv()
-    for step in range(1, NY):
-        to = lax.rem(y + step, NY)
-        y_send0[step - 1] = part0[core, to] + from_core0[to]
-        y_copy0(step).start()
 
     sublane = lax.broadcasted_iota(jnp.int32, (8, LANE), 0)
 
@@ -242,20 +266,16 @@
         total = part[q, core, y] + from_core[q, y]
         for step in range(1, NY):
             total = total + y_recv[q, step - 1].astype(F32)
-        proj[pl.ds(1, 2), :, pl.ds(q * HALF, HALF)] = total
-
-    after = at_ctx(lax.rem(ctx + 1, NCTX))
-    finish_inner(1)
+        proj[pl.ds(1, 2), :, pl.ds(q * PART, PART)] = total
+
+    finish_inner(order[0])
     halo_copy = remote(proj.at[pl.ds(1, 2), :, pl.ds(TOK - LANE, LANE)], halo, halo_send.at[0], halo_recv.at[0], after)
     halo_copy.start()
 
-    for n in (6, 7, 8):
-        loads[n].wait()
-    h_copies = all_of(filt_rows, h_rows, 0)
-    h_copies.wait_recv()
-    spec[...] = forward_transform(h_rows[...], first, mid, twist) * (2.0 / 65536)
-
-    finish_inner(0)
+    wait_plane()
+    exchange(filt_rows, h_rows, 0)
+    for q in order[1:]:
+        finish_inner(q)
     halo_copy.wait_recv()
     has_past = (ctx > 0).astype(F32)
 
@@ -272,6 +292,25 @@
     to_rows(carried[...], car_rows)
     exchange(car_rows, x_rows, 1)
 
+    core_copy0.wait_recv()
+    for step in (2, 1, 3):
+        to = lax.rem(y + step, NY)
+        y_send0[step - 1] = part0[core, to] + from_core0[to]
+        y_copy0(step).start()
+    for load in loads[late + 2:]:
+        load.wait()
+    h_copies = all_of(filt_rows, h_rows, 0)
+    h_copies.wait_recv()
+    spec[...] = forward_transform(h_rows[...], first, mid, twist) * (2.0 / 65536)
+
+    x_copies = all_of(car_rows, x_rows, 1)
+    x_copies.wait_recv()
+    x_spec = forward_transform(x_rows[...], first, mid, twist)
+    xr, xi = x_spec[:, :LANE], x_spec[:, LANE:]
+    hr, hi = spec[:, pl.ds(0, LANE)], spec[:, pl.ds(LANE, LANE)]
+    y_rows[...] = inverse_transform(xr * hr - xi * hi, xr * hi + xi * hr, last, mid, twist)
+    exchange(y_rows, back_rows, 2)
+
     for step in range(1, NY):
         y_copy0(step).wait_recv()
     total0 = part0[core, y] + from_core0[y]
@@ -280,46 +319,41 @@
     proj[0] = total0
     halo_copy0 = remote(proj.at[0, :, pl.ds(TOK - LANE, LANE)], halo0, halo_send.at[1], halo_recv.at[1], after)
     halo_copy0.start()
-
-    loads[9].wait()
-    x_copies = all_of(car_rows, x_rows, 1)
-    x_copies.wait_recv()
-    x_spec = forward_transform(x_rows[...], first, mid, twist)
-    xr, xi = x_spec[:, :LANE], x_spec[:, LANE:]
-    hr, hi = spec[:, pl.ds(0, LANE)], spec[:, pl.ds(LANE, LANE)]
-    y_rows[...] = inverse_transform(xr * hr - xi * hi, xr * hi + xi * hr, last, mid, twist)
-    exchange(y_rows, back_rows, 2)
-
     halo_copy0.wait_recv()
     feat0[...] = featured(0, halo0[...])
     y_copies = all_of(y_rows, back_rows, 2)
     y_copies.wait_recv()
-    for g in range(CH // 8):
-        for a in range(8):
-            rows, lanes = pl.ds(8 * g, 8), pl.ds(LANE * a, LANE)
-            conv = back_rows[pl.ds(64 * g + a, 8, stride=8), :]
-            feat0[rows, lanes] = feat0[rows, lanes] * (conv + cols[9, rows, :] * carried[rows, lanes])
-    out_ref[ch] = feat0[...].astype(BF)
-
-    def gather(slot, send, device):
-        return remote(out_ref.at[slot], out_ref.at[slot], g_send.at[send], g_recv.at[send], device)
-
-    sends = [gather(ch, step - 1, at_y(step)) for step in range(1, NY)]
-    sends.append(gather(ch, 3, partner))
-    for copy in sends:
-        copy.start()
-    for step in range(1, NY):
+    def gather(q, slot, send, device):
+        tile = out_ref.at[slot, :, pl.ds(q * PIECE, PIECE)]
+        return remote(tile, tile, g_send.at[q, send], g_recv.at[q, send], device)
+
+    sends = []
+    for q in range(PIECES):
+        for g in range(CH // 8):
+            for a in range(q * PIECE // LANE, (q + 1) * PIECE // LANE):
+                rows, lanes = pl.ds(8 * g, 8), pl.ds(LANE * a, LANE)
+                conv = back_rows[pl.ds(64 * g + a, 8, stride=8), :]
+                feat0[rows, lanes] = feat0[rows, lanes] * (conv + cols[9, rows, :] * carried[rows, lanes])
+        lanes = pl.ds(q * PIECE, PIECE)
+        out_ref[ch, :, lanes] = feat0[:, lanes].astype(BF)
+        sends.append(gather(q, ch, 1, at_y(2)))
+        sends[-1].start()
+    for q in range(PIECES):
+        for step, device in ((1, at_y(1)), (3, at_y(3)), (4, partner)):
+            sends.append(gather(q, ch, step - 1, device))
+            sends[-1].start()
+    for q, step in [(q, 2) for q in range(PIECES)] + [(q, step) for q in range(PIECES) for step in (1, 3)]:
         came = lax.rem(y + NY - step, NY) * 2 + core
-        gather(came, step - 1, at_y(step)).wait_recv()
-        passed = gather(came, 3 + step, partner)
-        passed.start()
-        sends.append(passed)
-    for send in range(3, 7):
-        gather(ch, send, partner).wait_recv()
+        gather(q, came, step - 1, at_y(step)).wait_recv()
+        sends.append(gather(q, came, 3 + step, partner))
+        sends[-1].start()
+    for q in range(PIECES):
+        for send in range(3, 7):
+            gather(q, ch, send, partner).wait_recv()
 
     for copy in sends:
         copy.wait_send()
-    for q in range(2):
+    for q in order:
         core_copy(q).wait_send()
         for step in range(1, NY):
             y_copy(q, step).wait_send()
@@ -339,25 +373,25 @@
     scratch = [
         vmem((TOK, 1024), BF), vmem((3, 1024, 256), BF), vmem((3, 256, 1024), BF), vmem((CH, TOK), F32),
         vmem(first.shape, BF), vmem(last.shape, BF), vmem(mid.shape, BF), vmem(twist.shape, F32),
-        vmem((2, 2, NY, 2, CH, HALF), F32), vmem((2, NY, 2, CH, HALF), F32),
-        vmem((2, NY - 1, 2, CH, HALF), BF), vmem((2, NY - 1, 2, CH, HALF), BF),
+        vmem((PARTS, 2, NY, 2, CH, PART), F32), vmem((PARTS, NY, 2, CH, PART), F32),
+        vmem((PARTS, NY - 1, 2, CH, PART), BF), vmem((PARTS, NY - 1, 2, CH, PART), BF),
         vmem((2, NY, CH, TOK), F32), vmem((NY, CH, TOK), F32),
         vmem((NY - 1, CH, TOK), F32), vmem((NY - 1, CH, TOK), F32),
         vmem((3, CH, TOK), F32), vmem((2, CH, LANE), F32), vmem((CH, LANE), F32), vmem((10, CH, LANE), F32),
         vmem((CH, TOK), F32), vmem((ROWS, LANE), F32), vmem((ROWS, LANE), F32), vmem((ROWS, LANE), F32),
         vmem((ROWS, LANE), F32), vmem((ROWS, 2 * LANE), F32), vmem((ROWS, LANE), F32), vmem((ROWS, LANE), F32),
         vmem((CH, TOK), F32),
-        dma((10,)), dma((3,)), dma((3,)), dma((3, 3)), dma((3, 3)), dma((2,)), dma((2,)), dma((3,)), dma((3,)),
-        dma((7,)), dma((7,)),
+        dma((8 + PARTS,)), dma((PARTS + 1,)), dma((PARTS + 1,)), dma((PARTS + 1, 3)), dma((PARTS + 1, 3)), dma((2,)), dma((2,)), dma((3,)), dma((3,)),
+        dma((PIECES, 7)), dma((PIECES, 7)), pltpu.SemaphoreType.REGULAR((2,)),
     ]
     return pl.pallas_call(
         kernel,
-        out_shape=jax.ShapeDtypeStruct((8, CH, TOK), BF),
+        out_shape=pltpu.VMEM((8, CH, TOK), BF),
         in_specs=[hbm, hbm, smem, hbm, smem, hbm, hbm, hbm, hbm],
         out_specs=pl.BlockSpec(memory_space=pltpu.VMEM),
         scratch_shapes=scratch,
         compiler_params=pltpu.CompilerParams(
-            collective_id=0, has_side_effects=True, vmem_limit_bytes=63 << 20
+            collective_id=0, has_side_effects=True, vmem_limit_bytes=62 << 20
         ),
         name="hyena",
     )(tokens, in_proj, jnp.transpose(short_taps, (1, 2, 0)), long_filter, skip_gain, first, last, mid, twist)

time: 48.9 us -> 43.1 us (0.88)
  Pallas kernels: 45.6 us -> 41 us
  matrix products: 3.11 us -> 2.07 us
    pallas_call x1, Pallas kernels: 45.6 us -> 41 us  [gated_values(): pl.pallas_call(kernel, out_shape=pltpu.VMEM((8, CH, TOK), BF), in_specs=[...]
    dot_general x1, matrix products: 3.11 us -> 2.07 us  [per_device(): jnp.einsum('ct,cd->td', gated, out_proj, preferred_element_type=F32)]
where the time goes in v2:
time: 43.1 us; the launch traced here: 43 us
  Pallas kernels  41 us (95%)
  matrix products  2.07 us (5%)
    pallas_call x1, Pallas kernels, gated_values(): pl.pallas_call(kernel, out_shape=pltpu.VMEM((8, CH, TOK), BF), in_specs=[...  41 us
    dot_general x1, matrix products, per_device(): jnp.einsum('ct,cd->td', gated, out_proj, preferred_element_type=F32)  2.07 us

profile of v2, /device:TPU:1, one launch (start us, length us, event | category | flops | bytes accessed | tf_op | source)
XLA Modules:
  0.0 43.0 jit_solution(11635999850415641845)
XLA Ops:
  0.0 0.0 copy-start
  0.0 41.0 %hyena.1 = bf16[8,32,1024]{2,1,0:T(8,128)(2,1)S(1)} custom-call(bf16[1024,1024]{1,0:T(8,128)(2,1)} %tok_hbm.1, bf16[3,1024,256]{2,1,0:T(8,128)(2,1)} %w_hbm.1, f32[3,3,32]{2,1,0:T(4,128)} %bitcast.5, f32[32,1024]{1,0:T(8,128)} %filt_hbm.1, f32[32]{0:T(128)} %skip.1, bf16[2,512,256]{2,1,0:T(8,128)(2,1)} %constant.8.clone.first_hbm, ...), custom_call_target="tpu_custom_call" | custom-call | tf_op jit(solution)/shard_map/hyena/pallas_call | solution.py:387
  41.0 0.0 copy-done
  41.0 2.1 %convolution_convert_fusion = bf16[1024,1024]{1,0:T(8,128)(2,1)} fusion(bf16[256,1024]{1,0:T(8,128)(2,1)S(1)} %bitcast.4, bf16[256,1024]{1,0:T(8,128)(2,1)S(1)} %copy-done), kind=kOutput, calls=%fused_computation | convolution fusion | flops 537919488 | bytes 3145728 | tf_op jit(solution)/shard_map/ct,cd->td/dot_general | solution.py:402
Async XLA Ops:
  0.0 41.0 %copy-start = (bf16[256,1024]{1,0:T(8,128)(2,1)S(1)}, bf16[256,1024]{1,0:T(8,128)(2,1)}, u32[]{:S(2)}) copy-start(bf16[256,1024]{1,0:T(8,128)(2,1)} %param.15) | copy-start | bytes 1572868

commit v3 on v2

--- a/solution.py
+++ b/solution.py
@@ -19,8 +19,6 @@
 PARTS = 4
 PART = TOK // PARTS
 HALF = TOK // 2
-PIECES = 1
-PIECE = TOK // PIECES
 ROWS = 256
 LANE = 128
 
@@ -102,6 +100,9 @@
     def at_y(step):
         return {"ctx": ctx, "ch": lax.rem(y + step, NY) * 2 + core}
 
+    def other_at_y(step):
+        return {"ctx": ctx, "ch": lax.rem(y + step, NY) * 2 + 1 - core}
+
     partner = {"ctx": ctx, "ch": y * 2 + 1 - core}
 
     def at_ctx(index):
@@ -143,7 +144,7 @@
 
     near = [at_y(2), at_y(1), at_y(3), along_z(2), along_z(6), along_x(2), along_z(1), along_z(7), along_x(1), along_x(3)]
     after, before = at_ctx(lax.rem(ctx + 1, NCTX)), at_ctx(lax.rem(ctx + NCTX - 1, NCTX))
-    near += [partner, after, before]
+    near += [partner, after, before, other_at_y(1), other_at_y(3)]
     for device in near:
         signal(barrier, device)
 
@@ -205,10 +206,10 @@
         return remote(src.at[others], dst.at[others], a2a_send.at[slot], a2a_recv.at[slot],
                       at_ctx(lax.rem(ctx + 1, NCTX)))
 
-    def to_rows(value, dst):
+    def to_rows(value, dst, blocks):
         for g in range(CH // 8):
-            for a in range(8):
-                dst[pl.ds(64 * g + a, 8, stride=8), :] = value[8 * g:8 * g + 8, LANE * a:LANE * a + LANE]
+            for n, a in enumerate(blocks):
+                dst[pl.ds(64 * g + a, 8, stride=8), :] = value[8 * g:8 * g + 8, LANE * n:LANE * n + LANE]
 
     def send_chip_sums(q):
         core_copy(q).wait_recv()
@@ -231,8 +232,36 @@
         core_copy(q).start()
         if n > 0:
             send_chip_sums(order[n - 1])
+    greet_plane()
     send_chip_sums(order[-1])
-    greet_plane()
+    loads[late].wait()
+    to_rows(filt[...], filt_rows, range(TOK // LANE))
+
+    sublane = lax.broadcasted_iota(jnp.int32, (8, LANE), 0)
+
+    def column(read, slot):
+        for g in range(CH // 8):
+            value = jnp.full((8, LANE), read(8 * g), F32)
+            for r in range(1, 8):
+                value = jnp.where(sublane == r, read(8 * g + r), value)
+            cols[slot, pl.ds(8 * g, 8), :] = value
+
+    for j in range(3):
+        for lag in range(3):
+            column(lambda c, j=j, lag=lag: taps[j, lag, c], 3 * j + lag)
+    column(lambda c: skip[c], 9)
+
+    def finish_inner(q):
+        for step in range(1, NY):
+            y_copy(q, step).wait_recv()
+        total = part[q, core, y] + from_core[q, y]
+        for step in range(1, NY):
+            total = total + y_recv[q, step - 1].astype(F32)
+        proj[pl.ds(1, 2), :, pl.ds(q * PART, PART)] = total
+
+    finish_inner(order[0])
+    halo_copy = remote(proj.at[pl.ds(1, 2), :, pl.ds(TOK - LANE, LANE)], halo, halo_send.at[0], halo_recv.at[0], after)
+    halo_copy.start()
 
     loads[late + 1].wait()
     transpose_weights(0)
@@ -242,54 +271,32 @@
             part0[k % 2, k // 2, :, pl.ds(q * HALF, HALF)] = value[k * CH:(k + 1) * CH]
     core_copy0 = remote(part0.at[1 - core], from_core0, core_send.at[PARTS], core_recv.at[PARTS], partner)
     core_copy0.start()
-
-    loads[late].wait()
-    to_rows(filt[...], filt_rows)
-
-    sublane = lax.broadcasted_iota(jnp.int32, (8, LANE), 0)
-
-    def column(read, slot):
-        for g in range(CH // 8):
-            value = jnp.full((8, LANE), read(8 * g), F32)
-            for r in range(1, 8):
-                value = jnp.where(sublane == r, read(8 * g + r), value)
-            cols[slot, pl.ds(8 * g, 8), :] = value
-
-    for j in range(3):
-        for lag in range(3):
-            column(lambda c, j=j, lag=lag: taps[j, lag, c], 3 * j + lag)
-    column(lambda c: skip[c], 9)
-
-    def finish_inner(q):
-        for step in range(1, NY):
-            y_copy(q, step).wait_recv()
-        total = part[q, core, y] + from_core[q, y]
-        for step in range(1, NY):
-            total = total + y_recv[q, step - 1].astype(F32)
-        proj[pl.ds(1, 2), :, pl.ds(q * PART, PART)] = total
-
-    finish_inner(order[0])
-    halo_copy = remote(proj.at[pl.ds(1, 2), :, pl.ds(TOK - LANE, LANE)], halo, halo_send.at[0], halo_recv.at[0], after)
-    halo_copy.start()
-
     wait_plane()
     exchange(filt_rows, h_rows, 0)
+
+
+    has_past = (ctx > 0).astype(F32)
+
+    def featured(j, q, first_past):
+        past = first_past * has_past if q == 0 else proj[j, :, pl.ds(q * PART - LANE, LANE)]
+        extended = jnp.concatenate([past, proj[j, :, pl.ds(q * PART, PART)]], axis=1)
+        total = jnp.zeros((CH, PART), F32)
+        for lag in range(3):
+            moved = extended if lag == 0 else pltpu.roll(extended, lag, 1)
+            tap = jnp.concatenate([cols[3 * j + lag]] * (PART // LANE), axis=1)
+            total = total + tap * moved[:, LANE:]
+        return total
+
+    def carry(q):
+        value = featured(1, q, halo[0]) * featured(2, q, halo[1])
+        carried[:, pl.ds(q * PART, PART)] = value
+        to_rows(value, car_rows, range(q * PART // LANE, (q + 1) * PART // LANE))
+
     for q in order[1:]:
         finish_inner(q)
+        carry(q + 1)
     halo_copy.wait_recv()
-    has_past = (ctx > 0).astype(F32)
-
-    def featured(j, past):
-        extended = jnp.concatenate([past * has_past, proj[j]], axis=1)
-        total = jnp.zeros((CH, TOK), F32)
-        for lag in range(3):
-            moved = extended if lag == 0 else pltpu.roll(extended, lag, 1)
-            tap = jnp.concatenate([cols[3 * j + lag]] * (TOK // LANE), axis=1)
-            total = total + tap * moved[:, LANE:]
-        return total
-
-    carried[...] = featured(1, halo[0]) * featured(2, halo[1])
-    to_rows(carried[...], car_rows)
+    carry(0)
     exchange(car_rows, x_rows, 1)
 
     core_copy0.wait_recv()
@@ -320,36 +327,36 @@
     halo_copy0 = remote(proj.at[0, :, pl.ds(TOK - LANE, LANE)], halo0, halo_send.at[1], halo_recv.at[1], after)
     halo_copy0.start()
     halo_copy0.wait_recv()
-    feat0[...] = featured(0, halo0[...])
+    for q in range(PARTS):
+        feat0[:, pl.ds(q * PART, PART)] = featured(0, q, halo0[...])
     y_copies = all_of(y_rows, back_rows, 2)
     y_copies.wait_recv()
-    def gather(q, slot, send, device):
-        tile = out_ref.at[slot, :, pl.ds(q * PIECE, PIECE)]
-        return remote(tile, tile, g_send.at[q, send], g_recv.at[q, send], device)
-
-    sends = []
-    for q in range(PIECES):
-        for g in range(CH // 8):
-            for a in range(q * PIECE // LANE, (q + 1) * PIECE // LANE):
-                rows, lanes = pl.ds(8 * g, 8), pl.ds(LANE * a, LANE)
-                conv = back_rows[pl.ds(64 * g + a, 8, stride=8), :]
-                feat0[rows, lanes] = feat0[rows, lanes] * (conv + cols[9, rows, :] * carried[rows, lanes])
-        lanes = pl.ds(q * PIECE, PIECE)
-        out_ref[ch, :, lanes] = feat0[:, lanes].astype(BF)
-        sends.append(gather(q, ch, 1, at_y(2)))
+    for g in range(CH // 8):
+        for a in range(TOK // LANE):
+            rows, lanes = pl.ds(8 * g, 8), pl.ds(LANE * a, LANE)
+            conv = back_rows[pl.ds(64 * g + a, 8, stride=8), :]
+            feat0[rows, lanes] = feat0[rows, lanes] * (conv + cols[9, rows, :] * carried[rows, lanes])
+    out_ref[ch] = feat0[...].astype(BF)
+
+    whole, upper, lower = pl.ds(0, CH), pl.ds(0, CH // 2), pl.ds(CH // 2, CH // 2)
+
+    def gather(slot, rows, lane, device):
+        tile = out_ref.at[slot, rows, :]
+        return remote(tile, tile, g_send.at[lane], g_recv.at[lane], device)
+
+    sends = [gather(ch, whole, 0, at_y(2)), gather(ch, upper, 1, at_y(1)), gather(ch, upper, 2, at_y(3))]
+    sends += [gather(ch, lower, 3, at_y(1)), gather(ch, lower, 4, at_y(3))]
+    sends += [gather(ch, lower, 5, other_at_y(1)), gather(ch, lower, 6, other_at_y(3)), gather(ch, whole, 7, partner)]
+    for copy in sends:
+        copy.start()
+    for step, lane, rows in ((1, 1, upper), (3, 2, upper), (2, 0, whole)):
+        came = lax.rem(y + NY - step, NY) * 2 + core
+        gather(came, rows, lane, partner).wait_recv()
+        sends.append(gather(came, rows, 8 + lane, partner))
         sends[-1].start()
-    for q in range(PIECES):
-        for step, device in ((1, at_y(1)), (3, at_y(3)), (4, partner)):
-            sends.append(gather(q, ch, step - 1, device))
-            sends[-1].start()
-    for q, step in [(q, 2) for q in range(PIECES)] + [(q, step) for q in range(PIECES) for step in (1, 3)]:
-        came = lax.rem(y + NY - step, NY) * 2 + core
-        gather(q, came, step - 1, at_y(step)).wait_recv()
-        sends.append(gather(q, came, 3 + step, partner))
-        sends[-1].start()
-    for q in range(PIECES):
-        for send in range(3, 7):
-            gather(q, ch, send, partner).wait_recv()
+    for lane, rows in enumerate((whole, upper, upper, lower, lower, lower, lower, whole, whole, upper, upper)):
+        if lane > 2:
+            gather(ch, rows, lane, partner).wait_recv()
 
     for copy in sends:
         copy.wait_send()
@@ -382,7 +389,7 @@
         vmem((ROWS, LANE), F32), vmem((ROWS, 2 * LANE), F32), vmem((ROWS, LANE), F32), vmem((ROWS, LANE), F32),
         vmem((CH, TOK), F32),
         dma((8 + PARTS,)), dma((PARTS + 1,)), dma((PARTS + 1,)), dma((PARTS + 1, 3)), dma((PARTS + 1, 3)), dma((2,)), dma((2,)), dma((3,)), dma((3,)),
-        dma((PIECES, 7)), dma((PIECES, 7)), pltpu.SemaphoreType.REGULAR((2,)),
+        dma((11,)), dma((11,)), pltpu.SemaphoreType.REGULAR((2,)),
     ]
     return pl.pallas_call(
         kernel,
@@ -397,9 +404,33 @@
     )(tokens, in_proj, jnp.transpose(short_taps, (1, 2, 0)), long_filter, skip_gain, first, last, mid, twist)
 
 
+OUT_BLOCKS = 4
+
+
+def project_out(gated, weights, out_hbm, held, sems):
+    size = TOK // OUT_BLOCKS
+    copies = []
+    for n in range(OUT_BLOCKS):
+        rows = pl.ds(n * size, size)
+        held[rows, :] = dot(gated[:, rows], weights[...], ((0,), (0,))).astype(BF)
+        copies.append(pltpu.make_async_copy(held.at[rows, :], out_hbm.at[rows, :], sems.at[n]))
+        copies[-1].start()
+    for copy in copies:
+        copy.wait()
+
+
 def per_device(tokens, in_proj, short_taps, long_filter, skip_gain, out_proj):
     gated = gated_values(tokens, in_proj, short_taps, long_filter, skip_gain).reshape(8 * CH, TOK)
-    return jnp.einsum("ct,cd->td", gated, out_proj, preferred_element_type=F32).astype(BF)
+    vmem = pl.BlockSpec(memory_space=pltpu.VMEM)
+    return pl.pallas_call(
+        project_out,
+        out_shape=jax.ShapeDtypeStruct((TOK, out_proj.shape[1]), BF),
+        in_specs=[vmem, vmem],
+        out_specs=pl.BlockSpec(memory_space=pltpu.HBM),
+        scratch_shapes=[pltpu.VMEM((TOK, out_proj.shape[1]), BF), pltpu.SemaphoreType.DMA((OUT_BLOCKS,))],
+        compiler_params=pltpu.CompilerParams(vmem_limit_bytes=32 << 20),
+        name="project_out",
+    )(gated, out_proj)
 
 
 def solution(mesh):

time: 43.1 us -> 42.6 us (0.988)
  matrix products: 2.07 us -> 0 us
  Pallas kernels: 41 us -> 42.5 us
    dot_general x1 -> x0, matrix products: 2.07 us -> none  [per_device(): jnp.einsum('ct,cd->td', gated, out_proj, preferred_element_type=F32)]
    pallas_call x0 -> x1, Pallas kernels: none -> 1.68 us  [per_device(): pl.pallas_call(project_out, out_shape=jax.ShapeDtypeStruct((TOK, out_proj...]
where the time goes in v3:
time: 42.6 us; the launch traced here: 42.5 us
  Pallas kernels  42.5 us (100%)
    pallas_call x1, Pallas kernels, gated_values(): pl.pallas_call(kernel, out_shape=pltpu.VMEM((8, CH, TOK), BF), in_specs=[...  40.8 us
    pallas_call x1, Pallas kernels, per_device(): pl.pallas_call(project_out, out_shape=jax.ShapeDtypeStruct((TOK, out_proj...  1.68 us

profile of v3, /device:TPU:1, one launch (start us, length us, event | category | flops | bytes accessed | tf_op | source)
XLA Modules:
  0.0 42.5 jit_solution(3022847597543620979)
XLA Ops:
  0.0 0.0 copy-start
  0.0 40.8 %hyena.1 = bf16[8,32,1024]{2,1,0:T(8,128)(2,1)S(1)} custom-call(bf16[1024,1024]{1,0:T(8,128)(2,1)} %tok_hbm.1, bf16[3,1024,256]{2,1,0:T(8,128)(2,1)} %w_hbm.1, f32[3,3,32]{2,1,0:T(4,128)} %bitcast.3, f32[32,1024]{1,0:T(8,128)} %filt_hbm.1, f32[32]{0:T(128)} %skip.1, bf16[2,512,256]{2,1,0:T(8,128)(2,1)} %constant.8.clone.first_hbm, ...), custom_call_target="tpu_custom_call" | custom-call | tf_op jit(solution)/shard_map/hyena/pallas_call | solution.py:394
  40.8 0.0 copy-done
  40.8 1.7 %project_out.1 = bf16[1024,1024]{1,0:T(8,128)(2,1)} custom-call(bf16[256,1024]{1,0:T(8,128)(2,1)S(1)} %bitcast.2, bf16[256,1024]{1,0:T(8,128)(2,1)S(1)} %copy-done), custom_call_target="tpu_custom_call" | custom-call | tf_op jit(solution)/shard_map/project_out/pallas_call | solution.py:425
Async XLA Ops:
  0.0 40.8 %copy-start = (bf16[256,1024]{1,0:T(8,128)(2,1)S(1)}, bf16[256,1024]{1,0:T(8,128)(2,1)}, u32[]{:S(2)}) copy-start(bf16[256,1024]{1,0:T(8,128)(2,1)} %weights.1) | copy-start | bytes 1572868

commit v4 on v3

--- a/solution.py
+++ b/solution.py
@@ -192,7 +192,8 @@
     def hops(place):
         return min(place[0], NX - place[0]) + min(place[1], NZ - place[1])
 
-    far_first = sorted(((dx, dz) for dx in range(NX) for dz in range(NZ) if dx or dz), key=hops, reverse=True)
+    turns = (0, 1, NZ - 1, 2, NZ - 2, 3, NZ - 3, 4)
+    far_first = sorted(((dx, dz) for dx in (2, 1, 3, 0) for dz in turns if dx or dz), key=hops, reverse=True)
 
     def exchange(src, dst, slot):
         for dx, dz in far_first:

time: 42.6 us -> 42.4 us (level)
  no operation moved by 1% of the time
where the time goes in v4:
time: 42.4 us; the launch traced here: 42.3 us
  Pallas kernels  42.3 us (100%)
    pallas_call x1, Pallas kernels, gated_values(): pl.pallas_call(kernel, out_shape=pltpu.VMEM((8, CH, TOK), BF), in_specs=[...  40.6 us
    pallas_call x1, Pallas kernels, per_device(): pl.pallas_call(project_out, out_shape=jax.ShapeDtypeStruct((TOK, out_proj...  1.68 us

profile of v4, /device:TPU:1, one launch (start us, length us, event | category | flops | bytes accessed | tf_op | source)
XLA Modules:
  0.0 42.3 jit_solution(12076785299624126475)
XLA Ops:
  0.0 0.0 copy-start
  0.0 40.6 %hyena.1 = bf16[8,32,1024]{2,1,0:T(8,128)(2,1)S(1)} custom-call(bf16[1024,1024]{1,0:T(8,128)(2,1)} %tok_hbm.1, bf16[3,1024,256]{2,1,0:T(8,128)(2,1)} %w_hbm.1, f32[3,3,32]{2,1,0:T(4,128)} %bitcast.3, f32[32,1024]{1,0:T(8,128)} %filt_hbm.1, f32[32]{0:T(128)} %skip.1, bf16[2,512,256]{2,1,0:T(8,128)(2,1)} %constant.8.clone.first_hbm, ...), custom_call_target="tpu_custom_call" | custom-call | tf_op jit(solution)/shard_map/hyena/pallas_call | solution.py:395
  40.7 0.0 copy-done
  40.7 1.7 %project_out.1 = bf16[1024,1024]{1,0:T(8,128)(2,1)} custom-call(bf16[256,1024]{1,0:T(8,128)(2,1)S(1)} %bitcast.2, bf16[256,1024]{1,0:T(8,128)(2,1)S(1)} %copy-done), custom_call_target="tpu_custom_call" | custom-call | tf_op jit(solution)/shard_map/project_out/pallas_call | solution.py:426
Async XLA Ops:
  0.0 40.7 %copy-start = (bf16[256,1024]{1,0:T(8,128)(2,1)S(1)}, bf16[256,1024]{1,0:T(8,128)(2,1)}, u32[]{:S(2)}) copy-start(bf16[256,1024]{1,0:T(8,128)(2,1)} %weights.1) | copy-start | bytes 1572868
